TPU v7x, 512 devices: a whole 4x8x8 slice. The times are simulated.
512 devices in a mesh: hull: 256 (over x, y, z), fn: 2 (over core).
Axes of the slice: x: 4, y: 8, z: 8, core: 2. Of those that a mesh axis runs over, the one named last changes fastest.
Arguments:
- adj_rhs: float32 [4096, 64, 128], P('hull', 'fn'), may hold values from -6 to 6
- psi_init: float32 [4096, 64, 128], P('hull', 'fn'), may hold values from -6 to 6
- couple: bfloat16 [4096, 6, 128, 128], P('hull'), may hold values from -0.109375 to 0.109375
- diag_inv: bfloat16 [4096, 128, 128], P('hull')
- neighbours: int32 [4096, 6], P('hull'), may hold values from 0 to 4095, as said below
- sens: bfloat16 [4096, 16, 128], P('hull'), may hold values from -0.125 to 0.125
- owner: int32 [4096, 16], P('hull'), may hold values from 0 to 4095, as said below
Outputs:
- adjoint: float32 [4096, 64, 128], P('hull', 'fn')
- grad: float32 [4096, 64], P(('hull', 'fn'))
Inputs may be any that keep to these rules, and one draw needn't show every extreme that they name: `neighbours`: every neighbour of block row i lies within 2 block rows of i, and the distance 2 occurs. `owner`: the slots below 8 of block b name coordinates within 8 of b (coordinate b sits at block b's position along the hull), and the distance 8 occurs; the other slots may name any coordinate.
All inputs are finite; a program needn't handle non-finite values.
Results may differ from a plain program's by a relative error of at most 0.0049.
Values may be sent and summed in bfloat16 or wider, within the bound.
A program may use at most 64 MiB of HBM per device.

v0:
```python
import jax
import jax.numpy as jnp
from jax import lax
from jax.sharding import PartitionSpec as P

NCOORD = 4096
REACH = 2
SWEEPS = 3


def extended(block, sides, width):
    for axis, dim in sides:
        count = lax.axis_size(axis)
        forward = [(i, i + 1) for i in range(count - 1)]
        backward = [(target, source) for source, target in forward]
        low = lax.ppermute(
            lax.slice_in_dim(block, block.shape[dim] - width, None, axis=dim), axis, forward
        )
        high = lax.ppermute(lax.slice_in_dim(block, 0, width, axis=dim), axis, backward)
        block = jnp.concatenate([low, block, high], axis=dim)
    return block


def shards(adj_rhs, psi_init, couple, diag_inv, neighbours, sens, owner):
    blocks = adj_rhs.shape[0]
    offset = lax.axis_index("hull") * blocks - REACH
    positions = neighbours - offset
    adjoint = psi_init
    for sweep_step in range(SWEEPS):
        lagged = adjoint.astype(jnp.bfloat16)
        padded = extended(lagged, (("hull", 0),), REACH)
        nearby = jnp.take(padded, positions, axis=0)
        coupled = jnp.einsum("bkfr,bkrs->bfs", nearby, couple, preferred_element_type=jnp.float32)
        updated = (adj_rhs - coupled).astype(jnp.bfloat16)
        adjoint = jnp.einsum("bfr,brs->bfs", updated, diag_inv, preferred_element_type=jnp.float32)
    final = adjoint.astype(jnp.bfloat16)
    contributions = -jnp.einsum("bfr,bmr->bmf", final, sens, preferred_element_type=jnp.float32)
    width_local = contributions.shape[2]
    flat_terms = contributions.reshape(-1, width_local)
    share_rows = NCOORD // lax.axis_size("hull")
    partial_sums = jax.ops.segment_sum(flat_terms, owner.reshape(-1), num_segments=NCOORD)
    totals = lax.psum(partial_sums, "hull")
    owned = lax.dynamic_slice_in_dim(totals, lax.axis_index("hull") * share_rows, share_rows, 0)
    gradient = lax.all_to_all(owned, "fn", split_axis=0, concat_axis=1, tiled=True)
    return (adjoint, gradient)


def solution(mesh):
    return jax.shard_map(
        shards,
        mesh=mesh,
        in_specs=(
            P("hull", "fn", None),
            P("hull", "fn", None),
            P("hull", None, None, None),
            P("hull", None, None),
            P("hull", None),
            P("hull", None, None),
            P("hull", None),
        ),
        out_specs=(P("hull", "fn", None), P(("hull", "fn"), None)),
        check_vma=False,
    )
```

profile of v0, /device:TPU:1, one launch (start us, length us, event | category | flops | bytes accessed | tf_op | source)
XLA Modules:
  0.0 319.5 jit_solution(5923326892874427416)
XLA Ops:
  7.2 1.1 convert_element_type.21
  8.4 4.8 %collective-permute-start = (bf16[2,32,128]{2,1,0:T(8,128)(2,1)S(1)}, bf16[2,32,128]{2,1,0:T(8,128)(2,1)S(1)}, u32[]{:S(2)}, u32[]{:S(2)}) collective-permute-start(bf16[2,32,128]{2,1,0:T(8,128)(2,1)S(1)} %get-tuple-element.9), channel_id=1, source_target_pairs={{0,2},{2,4},{4,6},{6,8},{8,10},{10,12},{12,14},{14,16},{16,18},{18... | collective-permute-start | bytes 49160 | tf_op jit(solution)/shard_map/ppermute | solution.py:16
  13.2 1.3 collective-permute-start.1
  14.5 0.7 compare_and_fusion
  15.5 2.8 collective-permute-done.1
  18.3 1.6 gather_fusion
  19.9 2.1 convolution_convert_fusion.1
  22.1 4.0 %collective-permute-start.2 = (bf16[2,32,128]{2,1,0:T(8,128)(2,1)S(1)}, bf16[2,32,128]{2,1,0:T(8,128)(2,1)S(1)}, u32[]{:S(2)}, u32[]{:S(2)}) collective-permute-start(bf16[2,32,128]{2,1,0:T(8,128)(2,1)S(1)} %get-tuple-element.7), channel_id=1, source_target_pairs={{0,2},{2,4},{4,6},{6,8},{8,10},{10,12},{12,14},{14,16},{16,18},{18... | collective-permute-start | bytes 49160 | tf_op jit(solution)/shard_map/ppermute | solution.py:16
  26.1 1.3 collective-permute-start.3
  27.4 5.0 %collective-permute-done.3 = bf16[2,32,128]{2,1,0:T(8,128)(2,1)S(1)} collective-permute-done((bf16[2,32,128]{2,1,0:T(8,128)(2,1)S(1)}, bf16[2,32,128]{2,1,0:T(8,128)(2,1)S(1)}, u32[]{:S(2)}, u32[]{:S(2)}) %collective-permute-start.3) | collective-permute-done | bytes 16416 | tf_op jit(solution)/shard_map/ppermute | solution.py:19
  32.4 1.6 gather_fusion.1
  34.0 2.1 convolution_convert_fusion
  36.2 4.6 %collective-permute-start.4 = (bf16[2,32,128]{2,1,0:T(8,128)(2,1)S(1)}, bf16[2,32,128]{2,1,0:T(8,128)(2,1)S(1)}, u32[]{:S(2)}, u32[]{:S(2)}) collective-permute-start(bf16[2,32,128]{2,1,0:T(8,128)(2,1)S(1)} %get-tuple-element.5), channel_id=1, source_target_pairs={{0,2},{2,4},{4,6},{6,8},{8,10},{10,12},{12,14},{14,16},{16,18},{18... | collective-permute-start | bytes 49160 | tf_op jit(solution)/shard_map/ppermute | solution.py:16
  40.7 1.3 collective-permute-start.5
  42.1 3.1 collective-permute-done.5
  45.2 1.6 gather_fusion.2
  46.8 2.1 fusion.6
  49.0 1.1 convolution_negate_fusion
  50.0 2.8 scatter_custom_fusion
  52.9 248.7 %all-reduce.2.cloned.1.call-done = f32[4096,32]{1,0:T(8,128)} async-done(((f32[4096,32]{1,0:T(8,128)}), f32[4096,32]{1,0:T(8,128)}) %all-reduce.2.cloned.1.call-update) | async-done | bytes 524304 | tf_op jit(solution)/shard_map/psum | solution.py:42
  301.6 0.7 dynamic-slice_bitcast_fusion
  302.3 8.4 %all_to_all.19 = f32[2,1,256]{2,1,0:T(1,128)S(1)} all-to-all(f32[2,1,256]{2,1,0:T(1,128)S(1)} %reshape.72), channel_id=1, replica_groups=mesh['hull'=256,'fn'=2] {'fn'}, dimensions={0} | all-to-all | bytes 4096 | tf_op jit(solution)/shard_map/all_to_all | solution.py:44
  311.2 0.7 reduce
  312.0 0.7 all_to_all.17
  (26 shorter events, 1.2 us)
Async XLA Ops:
  7.2 12.8 %copy-start = (bf16[16,6,128,128]{3,2,1,0:T(8,128)(2,1)S(1)}, bf16[16,6,128,128]{3,2,1,0:T(8,128)(2,1)}, u32[]{:S(2)}) copy-start(bf16[16,6,128,128]{3,2,1,0:T(8,128)(2,1)} %param.11) | copy-start | bytes 9437188
  7.2 294.4 %all-reduce.2.cloned.1.call-start = ((), (), s32[]{:S(2)}) async-start(), calls=%async_computation.1 | async-start | bytes 4194304 | tf_op jit(solution)/shard_map/psum | solution.py:42
  8.4 7.1 %collective-permute-start = (bf16[2,32,128]{2,1,0:T(8,128)(2,1)S(1)}, bf16[2,32,128]{2,1,0:T(8,128)(2,1)S(1)}, u32[]{:S(2)}, u32[]{:S(2)}) collective-permute-start(bf16[2,32,128]{2,1,0:T(8,128)(2,1)S(1)} %get-tuple-element.9), channel_id=1, source_target_pairs={{0,2},{2,4},{4,6},{6,8},{8,10},{10,12},{12,14},{14,16},{16,18},{18... | collective-permute-start | bytes 49160 | tf_op jit(solution)/shard_map/ppermute | solution.py:16
  13.2 5.1 %collective-permute-start.1 = (bf16[2,32,128]{2,1,0:T(8,128)(2,1)S(1)}, bf16[2,32,128]{2,1,0:T(8,128)(2,1)S(1)}, u32[]{:S(2)}, u32[]{:S(2)}) collective-permute-start(bf16[2,32,128]{2,1,0:T(8,128)(2,1)S(1)} %get-tuple-element.10), channel_id=1, source_target_pairs={{2,0},{4,2},{6,4},{8,6},{10,8},{12,10},{14,12},{16,14},{18,16},{20... | collective-permute-start | bytes 49160 | tf_op jit(solution)/shard_map/ppermute | solution.py:19
  22.1 5.3 %collective-permute-start.2 = (bf16[2,32,128]{2,1,0:T(8,128)(2,1)S(1)}, bf16[2,32,128]{2,1,0:T(8,128)(2,1)S(1)}, u32[]{:S(2)}, u32[]{:S(2)}) collective-permute-start(bf16[2,32,128]{2,1,0:T(8,128)(2,1)S(1)} %get-tuple-element.7), channel_id=1, source_target_pairs={{0,2},{2,4},{4,6},{6,8},{8,10},{10,12},{12,14},{14,16},{16,18},{18... | collective-permute-start | bytes 49160 | tf_op jit(solution)/shard_map/ppermute | solution.py:16
  26.1 6.3 %collective-permute-start.3 = (bf16[2,32,128]{2,1,0:T(8,128)(2,1)S(1)}, bf16[2,32,128]{2,1,0:T(8,128)(2,1)S(1)}, u32[]{:S(2)}, u32[]{:S(2)}) collective-permute-start(bf16[2,32,128]{2,1,0:T(8,128)(2,1)S(1)} %get-tuple-element.8), channel_id=1, source_target_pairs={{2,0},{4,2},{6,4},{8,6},{10,8},{12,10},{14,12},{16,14},{18,16},{20... | collective-permute-start | bytes 49160 | tf_op jit(solution)/shard_map/ppermute | solution.py:19
  32.4 9.6 %copy-start.2 = (s32[16,16]{1,0:T(8,128)S(1)}, s32[16,16]{1,0:T(8,128)}, u32[]{:S(2)}) copy-start(s32[16,16]{1,0:T(8,128)} %param.15) | copy-start | bytes 3076
  36.2 6.0 %collective-permute-start.4 = (bf16[2,32,128]{2,1,0:T(8,128)(2,1)S(1)}, bf16[2,32,128]{2,1,0:T(8,128)(2,1)S(1)}, u32[]{:S(2)}, u32[]{:S(2)}) collective-permute-start(bf16[2,32,128]{2,1,0:T(8,128)(2,1)S(1)} %get-tuple-element.5), channel_id=1, source_target_pairs={{0,2},{2,4},{4,6},{6,8},{8,10},{10,12},{12,14},{14,16},{16,18},{18... | collective-permute-start | bytes 49160 | tf_op jit(solution)/shard_map/ppermute | solution.py:16
  40.7 4.5 %collective-permute-start.5 = (bf16[2,32,128]{2,1,0:T(8,128)(2,1)S(1)}, bf16[2,32,128]{2,1,0:T(8,128)(2,1)S(1)}, u32[]{:S(2)}, u32[]{:S(2)}) collective-permute-start(bf16[2,32,128]{2,1,0:T(8,128)(2,1)S(1)} %get-tuple-element.6), channel_id=1, source_target_pairs={{2,0},{4,2},{6,4},{8,6},{10,8},{12,10},{14,12},{16,14},{18,16},{20... | collective-permute-start | bytes 49160 | tf_op jit(solution)/shard_map/ppermute | solution.py:19
  49.0 263.7 %copy-start.1 = (f32[16,32,128]{2,1,0:T(8,128)}, f32[16,32,128]{2,1,0:T(8,128)S(1)}, u32[]{:S(2)}) copy-start(f32[16,32,128]{2,1,0:T(8,128)S(1)} %fusion.6) | copy-start | bytes 786436
Sparse Core Ops, SparseCore 0:
  53.0 248.5 all-reduce.1
where the time goes:
time: 320 us
  waiting for transfers between devices  260 us (81%)
  starting transfers between devices  17.3 us (5%)
  between operations  14.2 us (4%)
  blocking collectives  8.39 us (3%)
  matrix products  7.47 us (2%)
  local copies, waits for them, and re-layouts  7.14 us (2%)
  other arithmetic  5.37 us (2%)
    psum x1, waiting for transfers between devices, shards(): totals = lax.psum(partial_sums, 'hull')  249 us
    ppermute x3, starting transfers between devices, extended(): lax.ppermute(lax.slice_in_dim(block, block.shape[dim] - width, None, axis...  13.4 us
    ppermute x3, waiting for transfers between devices, extended(): lax.ppermute(lax.slice_in_dim(block, 0, width, axis=dim), axis, backward)  11 us
    all_to_all x1, blocking collectives, shards(): lax.all_to_all(owned, 'fn', split_axis=0, concat_axis=1, tiled=True)  8.39 us
  transfers between devices with their start and end apart: 7, of which 4 were waited for; matrix products, arithmetic and copies ran while one was open for 0% of the time, Pallas kernels for 0%

commit v1 on v0

v1 whole, which is shorter than its diff:
```python
import functools

import jax
import jax.numpy as jnp
from jax import lax
from jax.experimental import pallas as pl
from jax.experimental.pallas import tpu as pltpu
from jax.sharding import PartitionSpec as P

MESH = pl.DeviceIdType.MESH
BF, F32, I32 = jnp.bfloat16, jnp.float32, jnp.int32
NX, NY, NZ = 4, 8, 8
B = 16
FN = 32
R = 128
NBR, KLOC, SWEEPS, REACH = 6, 16, 3, 2
GROUPS = ((2, 6), (6, 10), (10, 14), (0, 2), (14, 16))


def dot(a, b):
    return jnp.dot(a, b, preferred_element_type=F32)


def iota(shape, dim):
    return lax.broadcasted_iota(I32, shape, dim)


def lane_of(coordinate):
    y = (coordinate // (NZ * 16)) % NY
    core = (coordinate >> 3) & 1
    return (coordinate & 3) * 32 + y * 4 + core * 2 + ((coordinate >> 2) & 1)


def kernel(
    rhs_hbm, psi_hbm, couple_hbm, diag_hbm, nbr_hbm, sens_hbm, owner_hbm,
    adj_hbm, grad_ref,
    rhs, psi, couple, diag, nbr, sens, owner, adj,
    local0, local1, local2, edge0, edge1, edge2, st, tgt, oh, ohn, crecv, nsend, nrecv, dsend, xrecv, psend, precv,
    load_sem, weight_sem, out_sem, halo_s, halo_r, tgt_s, tgt_r, c_s, c_r, n_s, n_r, x_s, x_r, p_s, p_r,
):
    local, edge = (local0, local1, local2), (edge0, edge1, edge2)
    h = lax.axis_index("hull")
    core = lax.axis_index("fn")
    n_hull = NX * NY * NZ
    x, y, z = h // (NY * NZ), (h // NZ) % NY, h % NZ

    def device(i, j, k, c):
        return ((i * NY + j) * NZ + k, c)

    right, left = ((h + 1) % n_hull, core), ((h + n_hull - 1) % n_hull, core)
    z_peers = [device(x, y, (z + k) % NZ, core) for k in range(1, NZ)]
    x_peers = [device((x + k) % NX, y, z, core) for k in range(1, NX)]
    yc = [(k, e) for e in range(2) for k in range(NY) if (k, e) != (0, 0)]
    yc_peers = [device(x, (y + k) % NY, z, (core + e) % 2) for k, e in yc]

    barrier = pltpu.get_barrier_semaphore()
    everyone = [right, left] + z_peers + x_peers + yc_peers
    for peer in everyone:
        pl.semaphore_signal(barrier, inc=1, device_id=peer, device_id_type=MESH)

    loads = {}

    def load(name, source, target):
        loads[name] = pltpu.make_async_copy(source, target, load_sem.at[len(loads)])
        loads[name].start()

    load("psi0", psi_hbm.at[pl.ds(0, 2)], psi.at[pl.ds(0, 2)])
    load("psi1", psi_hbm.at[pl.ds(B - 2, 2)], psi.at[pl.ds(B - 2, 2)])
    load("owner", owner_hbm, owner)
    load("psi", psi_hbm.at[pl.ds(2, B - 4)], psi.at[pl.ds(2, B - 4)])
    load("nbr", nbr_hbm, nbr)
    load("rhs", rhs_hbm, rhs)
    weights = []
    for g, (a, b) in enumerate(GROUPS):
        rows = pl.ds(a, b - a)
        weights.append((
            pltpu.make_async_copy(couple_hbm.at[rows], couple.at[rows], weight_sem.at[2 * g]),
            pltpu.make_async_copy(diag_hbm.at[rows], diag.at[rows], weight_sem.at[2 * g + 1]),
        ))
        for copy in weights[-1]:
            copy.start()
        if g == 0:
            load("sens", sens_hbm, sens)

    def remote(source, target, send, recv, peer):
        copy = pltpu.make_async_remote_copy(
            src_ref=source, dst_ref=target, send_sem=send, recv_sem=recv, device_id=peer, device_id_type=MESH
        )
        copy.start()
        return copy

    def keep(s, i, value):
        local[s][i] = value
        if i < 4:
            edge[s][0, i + 2] = value
        if i >= B - 4:
            edge[s][1, i - (B - 4)] = value

    def send_halo(s):
        return (
            remote(local[s].at[pl.ds(B - 2, 2)], edge[s].at[0, pl.ds(0, 2)], halo_s.at[s, 0], halo_r.at[s, 0], right),
            remote(local[s].at[pl.ds(0, 2)], edge[s].at[1, pl.ds(4, 2)], halo_s.at[s, 1], halo_r.at[s, 1], left),
        )

    sent = []
    loads["psi0"].wait()
    loads["psi1"].wait()
    for i in (0, 1, B - 2, B - 1):
        keep(0, i, psi[i].astype(BF))
    loads["owner"].wait()
    owners = owner[...]
    slot, lane = iota((B, 128), 0), iota((B, 128), 1)
    high = (owners >> 6).astype(F32).astype(BF)
    low = (owners & 63).astype(F32).astype(BF)

    def owner_row(first):
        pick = jnp.where(slot == first + (lane & 7), 1.0, 0.0).astype(BF)
        spread = dot(high, pick) * 64.0 + dot(low, pick)
        return jnp.sum(jnp.where(slot == lane >> 3, spread, 0.0), axis=0, keepdims=True).astype(I32)

    tgt[0] = owner_row(8)
    near_owner = owner_row(0)

    pl.semaphore_wait(barrier, len(everyone))
    halo = send_halo(0)
    tgt_copies = [remote(tgt.at[0], tgt.at[k + 1], tgt_s.at[k], tgt_r.at[k], p) for k, p in enumerate(z_peers)]

    loads["psi"].wait()
    for i in range(2, B - 2):
        keep(0, i, psi[i].astype(BF))
    loads["nbr"].wait()
    loads["rhs"].wait()

    def block(s, i, read, first, count):
        nearby = [read(jnp.clip(nbr[k, i] - (h * B + first), 0, count - 1)) for k in range(NBR)]
        coupled = dot(jnp.concatenate(nearby, axis=1), couple[i].reshape(NBR * R, R))
        updated = (rhs[i] - coupled).astype(BF)
        return dot(updated, diag[i])

    def interior(s, i):
        return block(s, i, lambda p: local[s][p], 0, B)

    def boundary(s, i):
        side = 0 if i < 2 else 1
        return block(s, i, lambda p: edge[s][side, p], -2 if side == 0 else B - 4, 6)

    far, near = [], []

    def finish(i, value):
        adj[i] = value
        terms = dot(value.astype(BF), st[...])
        mine = iota((FN, 128), 1) >> 3 == i
        far.append(jnp.where(mine, terms[:, :128], 0.0))
        near.append(jnp.where(mine, terms[:, 128:], 0.0))

    outs = []

    def put(a, b):
        rows = pl.ds(a, b - a)
        outs.append(pltpu.make_async_copy(adj.at[rows], adj_hbm.at[rows], out_sem.at[len(outs)]))
        outs[-1].start()

    for s in range(SWEEPS):
        last = s == SWEEPS - 1
        for g, (a, b) in enumerate(GROUPS):
            if a == 0:
                if s == 0:
                    loads["sens"].wait()
                    wide = sens[...].astype(F32)
                    for q, first in enumerate((8, 0)):
                        part = wide[:, first:first + 8, :].reshape(128, R)
                        st[:, q * 128:(q + 1) * 128] = (-jnp.transpose(part)).astype(BF)
                    block_of = near_owner >> 4
                    group = jnp.where(block_of == h, 0, jnp.where(block_of == h - 1, 128, 256))
                    place = jnp.where(jnp.abs(block_of - h) <= 1, group + lane_of(near_owner), -1)
                    column = jnp.transpose(jnp.broadcast_to(place, (8, 128)).astype(F32))[:, :1].astype(I32)
                    ohn[...] = jnp.where(column == iota((128, 384), 1), 1.0, 0.0).astype(BF)
                if s == 1:
                    for copy in tgt_copies:
                        copy.wait_recv()
                    rows = jnp.concatenate([tgt[k] for k in range(NZ)], axis=0)
                    hull = rows >> 4
                    place = jnp.where(hull % NZ == z, (hull // (NY * NZ)) * 128 + lane_of(rows), -1)
                    if NZ < 8:
                        place = jnp.concatenate([place] * (8 // NZ), axis=0)
                    columns = jnp.transpose(place.astype(F32)).astype(I32)
                    for k in range(NZ):
                        oh[k * 128:(k + 1) * 128, :] = jnp.where(
                            columns[:, k:k + 1] == iota((128, NX * 128), 1), 1.0, 0.0
                        ).astype(BF)
                for copy in halo:
                    copy.wait_recv()
            if s == 0:
                for copy in weights[g]:
                    copy.wait()
            for i in range(a, b):
                value = boundary(s, i) if a == 0 or b == B else interior(s, i)
                if last:
                    finish(i, value)
                else:
                    keep(s + 1, i, value.astype(BF))
            if last and b == B - 2:
                put(2, B - 2)
        sent += halo
        if not last:
            halo = send_halo(s + 1)
    put(0, 2)
    put(B - 2, B)

    crecv[0] = sum(far).astype(BF)
    c_copies = [remote(crecv.at[0], crecv.at[k + 1], c_s.at[k], c_r.at[k], p) for k, p in enumerate(z_peers)]
    close = dot(sum(near).astype(BF), ohn[...])
    nsend[0] = close[:, 128:256]
    nsend[1] = close[:, 256:]
    n_copies = [remote(nsend.at[k], nrecv.at[k], n_s.at[k], n_r.at[k], p) for k, p in enumerate((left, right))]
    for copy in c_copies:
        copy.wait_recv()
    dense = dot(jnp.concatenate([crecv[k] for k in range(NZ)], axis=1), oh[...])

    for q in range(NX):
        dsend[q] = dense[:, q * 128:(q + 1) * 128]
    x_copies = [
        remote(dsend.at[(x + k + 1) % NX], xrecv.at[k], x_s.at[k], x_r.at[k], p) for k, p in enumerate(x_peers)
    ]
    for copy in n_copies:
        copy.wait_recv()
    total = close[:, :128] + nrecv[0] + nrecv[1] + dsend[x]
    for copy in x_copies:
        copy.wait_recv()
    for k in range(NX - 1):
        total = total + xrecv[k]

    stacked = jnp.concatenate([total if g == 0 else pltpu.roll(total, 128 - 32 * g, 1) for g in range(4)], axis=0)
    packed = jnp.transpose(stacked)
    for d in range(2 * NY):
        psend[d] = packed[2 * d:2 * d + 2, :]
    p_copies = [
        remote(
            psend.at[((y + k) % NY) * 2 + (core + e) % 2], precv.at[e * NY + k], p_s.at[m], p_r.at[m], yc_peers[m]
        )
        for m, (k, e) in enumerate(yc)
    ]
    own = psend[y * 2 + core]
    for copy in p_copies:
        copy.wait_recv()
    halves = []
    for e in range(2):
        half = own if e == 0 else precv[NY]
        for k in range(1, NY):
            half = half + precv[e * NY + k]
        halves.append(half)
    ordered = (jnp.where(core == 0, halves[0], halves[1]), jnp.where(core == 0, halves[1], halves[0]))
    row, lane = iota((8, 128), 0), iota((8, 128), 1)
    wide = [jnp.where(row < 4, half[0:1], half[1:2]) for half in ordered]
    result = jnp.zeros((8, 128), F32)
    for g in range(4):
        first = wide[0] if g == 0 else pltpu.roll(wide[0], 128 - 32 * g, 1)
        second = wide[1] if g == 1 else pltpu.roll(wide[1], (160 - 32 * g) % 128, 1)
        result = jnp.where((row & 3) == g, jnp.where(lane < FN, first, second), result)
    grad_ref[...] = result[:, :2 * FN]

    for copy in list(sent) + tgt_copies + c_copies + n_copies + x_copies + p_copies:
        copy.wait_send()
    for copy in outs:
        copy.wait()


def shards(adj_rhs, psi_init, couple, diag_inv, neighbours, sens, owner):
    vmem, dma = pltpu.VMEM, pltpu.SemaphoreType.DMA
    return pl.pallas_call(
        kernel,
        out_shape=(jax.ShapeDtypeStruct((B, FN, R), F32), jax.ShapeDtypeStruct((8, 2 * FN), F32)),
        in_specs=[pl.BlockSpec(memory_space=pl.ANY)] * 7,
        out_specs=(pl.BlockSpec(memory_space=pl.ANY), pl.BlockSpec(memory_space=pltpu.VMEM)),
        scratch_shapes=[
            vmem((B, FN, R), F32),
            vmem((B, FN, R), F32),
            vmem((B, NBR, R, R), BF),
            vmem((B, R, R), BF),
            pltpu.SMEM((NBR, B), I32),
            vmem((B, KLOC, R), BF),
            vmem((B, KLOC), I32),
            vmem((B, FN, R), F32),
            *[vmem((B, FN, R), BF)] * SWEEPS,
            *[vmem((2, 6, FN, R), BF)] * SWEEPS,
            vmem((R, 256), BF),
            vmem((NZ, 1, 128), I32),
            vmem((NZ * 128, NX * 128), BF),
            vmem((128, 384), BF),
            vmem((NZ, FN, 128), BF),
            vmem((2, FN, 128), F32),
            vmem((2, FN, 128), F32),
            vmem((NX, FN, 128), F32),
            vmem((NX - 1, FN, 128), F32),
            vmem((16, 2, 128), F32),
            vmem((2 * NY, 2, 128), F32),
            dma((7,)), dma((2 * len(GROUPS),)), dma((3,)),
            dma((SWEEPS, 2)), dma((SWEEPS, 2)),
            dma((NZ - 1,)), dma((NZ - 1,)), dma((NZ - 1,)), dma((NZ - 1,)),
            dma((2,)), dma((2,)),
            dma((NX - 1,)), dma((NX - 1,)),
            dma((2 * NY - 1,)), dma((2 * NY - 1,)),
        ],
        compiler_params=pltpu.CompilerParams(
            collective_id=0, has_side_effects=True, vmem_limit_bytes=63 * 2**20
        ),
        name="adjoint_gradient",
    )(adj_rhs, psi_init, couple, diag_inv, neighbours.T, sens, owner)


def solution(mesh):
    return jax.shard_map(
        shards,
        mesh=mesh,
        in_specs=(
            P("hull", "fn", None),
            P("hull", "fn", None),
            P("hull", None, None, None),
            P("hull", None, None),
            P("hull", None),
            P("hull", None, None),
            P("hull", None),
        ),
        out_specs=(P("hull", "fn", None), P(("hull", "fn"), None)),
        check_vma=False,
    )
```

time: 320 us -> 50.7 us (0.16)
  waiting for transfers between devices: 260 us -> 0 us
  Pallas kernels: 0 us -> 46.9 us
  starting transfers between devices: 17.3 us -> 0 us
  between operations: 14.2 us -> 0.64 us
  blocking collectives: 8.39 us -> 0 us
  matrix products: 7.47 us -> 0 us
  other arithmetic: 5.37 us -> 0 us
  local copies, waits for them, and re-layouts: 7.14 us -> 2.95 us
    psum x1 -> x0, waiting for transfers between devices: 249 us -> none  [shards(): totals = lax.psum(partial_sums, 'hull')]
    pallas_call x0 -> x1, Pallas kernels: none -> 46.9 us  [shards(): pl.pallas_call(kernel, out_shape=(jax.ShapeDtypeStruct((B, FN, R), F32),...]
    ppermute x6 -> x0, starting transfers between devices: 17.3 us -> none  [the longest x3 13.4 us: extended(): lax.ppermute(lax.slice_in_dim(block, block.shape[dim] - width, None, axis...]
    ppermute x6 -> x0, waiting for transfers between devices: 11 us -> none  [the longest x3 11 us: extended(): lax.ppermute(lax.slice_in_dim(block, 0, width, axis=dim), axis, backward)]
    all_to_all x1 -> x0, blocking collectives: 8.39 us -> none  [shards(): lax.all_to_all(owned, 'fn', split_axis=0, concat_axis=1, tiled=True)]
    dot_general x4 -> x0, matrix products: 7.47 us -> none  [the longest x3 6.4 us: shards(): jnp.einsum('bfr,brs->bfs', updated, diag_inv, preferred_element_type=jnp....]
    gather x3 -> x0, local copies, waits for them, and re-layouts: 4.71 us -> none  [shards(): nearby = jnp.take(padded, positions, axis=0)]
  transfers between devices with their start and end apart: 7 -> 0, of which waited for: 4 -> 0; matrix products, arithmetic and copies ran while one was open for 0% -> 0% of each run, Pallas kernels for 0% -> 0%
where the time goes in v1:
time: 50.7 us; the launch traced here: 50.5 us
  Pallas kernels  46.9 us (93%)
  local copies, waits for them, and re-layouts  2.95 us (6%)
  between operations  0.64 us (1%)
    pallas_call x1, Pallas kernels, shards(): pl.pallas_call(kernel, out_shape=(jax.ShapeDtypeStruct((B, FN, R), F32),...  46.9 us
    unnamed x2, local copies, waits for them, and re-layouts  2.95 us

profile of v1, /device:TPU:1, one launch (start us, length us, event | category | flops | bytes accessed | tf_op | source)
XLA Modules:
  0.0 50.5 jit_solution(14196268182422268360)
XLA Ops:
  0.6 46.9 %adjoint_gradient.1 = (f32[16,32,128]{2,1,0:T(8,128)}, f32[8,64]{1,0:T(8,128)}) custom-call(f32[16,32,128]{2,1,0:T(8,128)} %rhs_hbm.1, f32[16,32,128]{2,1,0:T(8,128)} %psi_hbm.1, bf16[16,6,128,128]{3,2,1,0:T(8,128)(2,1)} %couple_hbm.1, bf16[16,128,128]{2,1,0:T(8,128)(2,1)} %diag_hbm.1, s32[6,16]{1,0:T(8,128)} %bitcast.1, bf16[16,16,128]{2,1,0:T(8,128)(2,1)} %sens_hbm.1, ...), custom_call_target="tpu_custom_call" | custom-call | tf_op jit(solution)/shard_map/adjoint_gradient/pallas_call | solution.py:270
  47.6 1.7 %copy.11 = f32[16,32,128]{2,1,0:T(8,128)} copy(f32[16,32,128]{2,1,0:T(8,128)} %get-tuple-element.4) | data formatting | bytes 524288
  49.2 1.3 %copy.12 = f32[8,64]{1,0:T(8,128)} copy(f32[8,64]{1,0:T(8,128)} %get-tuple-element.5) | data formatting | bytes 4096

commit v2 on v1

v2 whole, which is shorter than its diff:
```python
import functools

import jax
import jax.numpy as jnp
from jax import lax
from jax.experimental import pallas as pl
from jax.experimental.pallas import tpu as pltpu
from jax.sharding import PartitionSpec as P

MESH = pl.DeviceIdType.MESH
BF, F32, I32 = jnp.bfloat16, jnp.float32, jnp.int32
NX, NY, NZ = 4, 8, 8
B = 16
FN = 32
R = 128
NBR, KLOC, SWEEPS, REACH = 6, 16, 3, 2
GROUPS = ((2, 6), (6, 10), (10, 14), (0, 2), (14, 16))
INNER = tuple(range(2, B - 2))
OUTER = (0, 1, B - 2, B - 1)


def dot(a, b):
    return jnp.dot(a, b, preferred_element_type=F32)


def iota(shape, dim):
    return lax.broadcasted_iota(I32, shape, dim)


def kernel(
    rhs_hbm, psi_hbm, couple_hbm, diag_hbm, nbr_hbm, sens_hbm, owner_hbm,
    adj_hbm, grad_ref,
    rhs, psi, couple, diag, nbr, sens, owner, adj,
    local0, local1, local2, edge0, edge1, edge2, st, tgt, oh, ohn, crecv, nsend, nrecv, psend, precv,
    load_sem, weight_sem, out_sem, halo_s, halo_r, tgt_s, tgt_r, c_s, c_r, n_s, n_r, p_s, p_r, plane_sem,
):
    local, edge = (local0, local1, local2), (edge0, edge1, edge2)
    h = lax.axis_index("hull")
    core = lax.axis_index("fn")
    n_hull = NX * NY * NZ
    x, y, z = h // (NY * NZ), (h // NZ) % NY, h % NZ

    def device(i, j, k, c):
        return ((i * NY + j) * NZ + k, c)

    has_left, has_right = h > 0, h < n_hull - 1
    left, right = (jnp.maximum(h - 1, 0), core), (jnp.minimum(h + 1, n_hull - 1), core)
    z_steps = sorted(range(1, NZ), key=lambda k: -min(k, NZ - k))
    z_peers = [device(x, y, (z + k) % NZ, core) for k in z_steps]
    x_peers = [device((x + k) % NX, y, z, core) for k in range(1, NX)]
    plane = [(e, i, k) for e in range(2) for i in range(NX) for k in range(NY) if (e, i, k) != (0, 0, 0)]
    plane.sort(key=lambda t: (-min(t[1], NX - t[1]) - min(t[2], NY - t[2]), -t[0]))
    plane_peers = [device((x + i) % NX, (y + k) % NY, z, (core + e) % 2) for e, i, k in plane]
    yc_peers = [p for p, (e, i, k) in zip(plane_peers, plane) if i == 0]

    barrier = pltpu.get_barrier_semaphore()
    everyone = z_peers + x_peers + yc_peers
    for there, peer in ((has_right, right), (has_left, left)):
        @pl.when(there)
        def _():
            pl.semaphore_signal(barrier, inc=1, device_id=peer, device_id_type=MESH)
    for peer in everyone:
        pl.semaphore_signal(barrier, inc=1, device_id=peer, device_id_type=MESH)

    loads = {}

    def load(name, source, target):
        loads[name] = pltpu.make_async_copy(source, target, load_sem.at[len(loads)])
        loads[name].start()

    load("psi0", psi_hbm.at[pl.ds(0, 2)], psi.at[pl.ds(0, 2)])
    load("psi1", psi_hbm.at[pl.ds(B - 2, 2)], psi.at[pl.ds(B - 2, 2)])
    load("owner", owner_hbm, owner)
    load("psi", psi_hbm.at[pl.ds(2, B - 4)], psi.at[pl.ds(2, B - 4)])
    load("nbr", nbr_hbm, nbr)
    load("rhs", rhs_hbm, rhs)
    weights = []
    for g, (a, b) in enumerate(GROUPS):
        rows = pl.ds(a, b - a)
        weights.append((
            pltpu.make_async_copy(couple_hbm.at[rows], couple.at[rows], weight_sem.at[2 * g]),
            pltpu.make_async_copy(diag_hbm.at[rows], diag.at[rows], weight_sem.at[2 * g + 1]),
        ))
        for copy in weights[-1]:
            copy.start()
        if g == 0:
            load("sens", sens_hbm, sens)

    def remote(source, target, send, recv, peer):
        copy = pltpu.make_async_remote_copy(
            src_ref=source, dst_ref=target, send_sem=send, recv_sem=recv, device_id=peer, device_id_type=MESH
        )
        copy.start()
        return copy

    def keep(s, i, value):
        local[s][i] = value
        if i < 4:
            edge[s][0, i + 2] = value
        if i >= B - 4:
            edge[s][1, i - (B - 4)] = value

    class Pair:
        def __init__(self, sources, targets, send, recv):
            self.copies = [
                pltpu.make_async_remote_copy(
                    src_ref=sources[k], dst_ref=targets[k], send_sem=send[k], recv_sem=recv[k],
                    device_id=(right, left)[k], device_id_type=MESH,
                )
                for k in range(2)
            ]

            @pl.when(has_right)
            def _():
                self.copies[0].start()

            @pl.when(has_left)
            def _():
                self.copies[1].start()

        def wait_recv(self):
            @pl.when(has_left)
            def _():
                self.copies[0].wait_recv()

            @pl.when(has_right)
            def _():
                self.copies[1].wait_recv()

        def wait_send(self):
            @pl.when(has_right)
            def _():
                self.copies[0].wait_send()

            @pl.when(has_left)
            def _():
                self.copies[1].wait_send()

    def send_halo(s):
        return Pair(
            (local[s].at[pl.ds(B - 2, 2)], local[s].at[pl.ds(0, 2)]),
            (edge[s].at[0, pl.ds(0, 2)], edge[s].at[1, pl.ds(4, 2)]),
            (halo_s.at[s, 0], halo_s.at[s, 1]),
            (halo_r.at[s, 0], halo_r.at[s, 1]),
        )

    @pl.when(jnp.logical_not(has_left))
    def _():
        for ref in edge:
            ref[0, 0:2] = jnp.zeros((2, FN, R), BF)
        nrecv[0] = jnp.zeros((FN, 128), F32)

    @pl.when(jnp.logical_not(has_right))
    def _():
        for ref in edge:
            ref[1, 4:6] = jnp.zeros((2, FN, R), BF)
        nrecv[1] = jnp.zeros((FN, 128), F32)

    sent = []
    loads["psi0"].wait()
    loads["psi1"].wait()
    for i in (0, 1, B - 2, B - 1):
        keep(0, i, psi[i].astype(BF))
    loads["owner"].wait()
    owners = owner[...]
    slot, lane = iota((B, 128), 0), iota((B, 128), 1)
    high = (owners >> 6).astype(F32).astype(BF)
    low = (owners & 63).astype(F32).astype(BF)

    def owner_row(first):
        pick = jnp.where(slot == first + (lane & 7), 1.0, 0.0).astype(BF)
        spread = dot(high, pick) * 64.0 + dot(low, pick)
        return jnp.sum(jnp.where(slot == lane >> 3, spread, 0.0), axis=0, keepdims=True).astype(I32)

    tgt[0] = owner_row(8)
    near_owner = owner_row(0)

    pl.semaphore_wait(barrier, len(everyone) + has_right.astype(I32) + has_left.astype(I32))
    for peer in x_peers:
        pl.semaphore_signal(plane_sem, inc=1, device_id=peer, device_id_type=MESH)
    halo = send_halo(0)
    tgt_copies = [remote(tgt.at[0], tgt.at[k], tgt_s.at[k - 1], tgt_r.at[k - 1], p) for k, p in zip(z_steps, z_peers)]

    loads["psi"].wait()
    for i in range(2, B - 2):
        keep(0, i, psi[i].astype(BF))

    def blocks(s, rows, read):
        updated = []
        for i in rows:
            nearby = jnp.concatenate([read(i, nbr[k, i] - h * B) for k in range(NBR)], axis=1)
            updated.append((rhs[i] - dot(nearby, couple[i].reshape(NBR * R, R))).astype(BF))
        return [dot(u, diag[i]) for u, i in zip(updated, rows)]

    def interior(s):
        return blocks(s, INNER, lambda i, p: local[s][jnp.clip(p, 0, B - 1)])

    def boundary(s):
        def read(i, p):
            if i < 2:
                return edge[s][0, jnp.clip(p + 2, 0, 5)]
            return edge[s][1, jnp.clip(p - (B - 4), 0, 5)]

        return blocks(s, OUTER, read)

    outs = []

    def put(a, b):
        rows = pl.ds(a, b - a)
        outs.append(pltpu.make_async_copy(adj.at[rows], adj_hbm.at[rows], out_sem.at[len(outs)]))
        outs[-1].start()

    def contributions(rows, values):
        terms = dot(jnp.concatenate([v.astype(BF) for v in values], axis=0), st[...])
        column = iota((FN, 256), 1) % 128 >> 3
        return sum(jnp.where(column == i, terms[FN * n:FN * (n + 1), :], 0.0) for n, i in enumerate(rows))

    loads["nbr"].wait()
    loads["rhs"].wait()
    for group in weights:
        for copy in group:
            copy.wait()
    for i, value in zip(INNER, interior(0)):
        keep(1, i, value.astype(BF))
    loads["sens"].wait()
    wide = sens[...].astype(F32)
    for q, first in enumerate((8, 0)):
        part = wide[:, first:first + 8, :].reshape(128, R)
        st[:, q * 128:(q + 1) * 128] = (-jnp.transpose(part)).astype(BF)
    block_of = near_owner >> 4
    group = jnp.where(block_of == h, 0, jnp.where(block_of == h - 1, 128, 256))
    place = group + (near_owner & 3) * 32 + ((near_owner >> 3) & 1) * 2 + ((near_owner >> 2) & 1)
    place = jnp.where(jnp.abs(block_of - h) <= 1, place, -1)
    column = jnp.transpose(jnp.broadcast_to(place, (8, 128)).astype(F32))[:, :1].astype(I32)
    ohn[...] = jnp.where(column == iota((128, 384), 1), 1.0, 0.0).astype(BF)

    for s in range(SWEEPS):
        last = s == SWEEPS - 1
        halo.wait_recv()
        sent.append(halo)
        values = boundary(s)
        if last:
            break
        for i, value in zip(OUTER, values):
            keep(s + 1, i, value.astype(BF))
        halo = send_halo(s + 1)
        inner = interior(s + 1)
        if s + 1 < SWEEPS - 1:
            for i, value in zip(INNER, inner):
                keep(s + 2, i, value.astype(BF))
            for copy in tgt_copies:
                copy.wait_recv()
            rows = jnp.concatenate([tgt[k] for k in range(NZ)], axis=0)
            hull = rows >> 4
            place = (rows & 3) * 128 + (hull // NZ) * 4 + ((rows >> 3) & 1) * 2 + ((rows >> 2) & 1)
            place = jnp.where(hull % NZ == z, place, -1)
            if NZ < 8:
                place = jnp.concatenate([place] * (8 // NZ), axis=0)
            columns = jnp.transpose(place.astype(F32)).astype(I32)
            for k in range(NZ):
                oh[k * 128:(k + 1) * 128, :] = jnp.where(columns[:, k:k + 1] == iota((128, 512), 1), 1.0, 0.0).astype(BF)
        else:
            for i, value in zip(INNER, inner):
                adj[i] = value
            put(2, B - 2)
            terms = contributions(INNER, inner)
    terms = terms + contributions(OUTER, values)

    terms = terms.astype(BF)
    crecv[0] = terms[:, :128]
    c_copies = [remote(crecv.at[0], crecv.at[k], c_s.at[k - 1], c_r.at[k - 1], p) for k, p in zip(z_steps, z_peers)]
    close = dot(terms[:, 128:], ohn[...])
    nsend[0] = close[:, 256:]
    nsend[1] = close[:, 128:256]
    n_copies = Pair(*[(ref.at[0], ref.at[1]) for ref in (nsend, nrecv, n_s, n_r)])
    for i, value in zip(OUTER, values):
        adj[i] = value
    put(0, 2)
    put(B - 2, B)
    n_copies.wait_recv()
    close = close[:, :128] + nrecv[0] + nrecv[1]
    stacked = jnp.concatenate([close if g == 0 else pltpu.roll(close, 128 - 32 * g, 1) for g in range(4)], axis=0)
    close = jnp.transpose(stacked)[:4, :]
    pl.semaphore_wait(plane_sem, NX - 1)
    for copy in c_copies:
        copy.wait_recv()
    dense = dot(jnp.concatenate([crecv[k] for k in range(NZ)], axis=1), oh[...])

    packed = jnp.transpose(jnp.concatenate([dense[:, g * 128:(g + 1) * 128] for g in range(4)], axis=0))
    for d in range(2 * NX * NY):
        psend[d] = packed[2 * d:2 * d + 2, :]
    mine = (x * NY + y) * 2
    psend[mine] += close[0:2, :]
    psend[mine + 1] += close[2:4, :]
    p_copies = [
        remote(
            psend.at[(((x + i) % NX) * NY + (y + k) % NY) * 2 + (core + e) % 2],
            precv.at[(e * NX + i) * NY + k], p_s.at[n], p_r.at[n], plane_peers[n],
        )
        for n, (e, i, k) in enumerate(plane)
    ]
    own = psend[mine + core]
    for copy in p_copies:
        copy.wait_recv()
    half = NX * NY
    halves = [own + jnp.sum(precv[1:half], axis=0), jnp.sum(precv[half:2 * half], axis=0)]
    ordered = (jnp.where(core == 0, halves[0], halves[1]), jnp.where(core == 0, halves[1], halves[0]))
    row, lane = iota((8, 128), 0), iota((8, 128), 1)
    wide = [jnp.where(row < 4, half[0:1], half[1:2]) for half in ordered]
    result = jnp.zeros((8, 128), F32)
    for g in range(4):
        first = wide[0] if g == 0 else pltpu.roll(wide[0], 128 - 32 * g, 1)
        second = wide[1] if g == 1 else pltpu.roll(wide[1], (160 - 32 * g) % 128, 1)
        result = jnp.where((row & 3) == g, jnp.where(lane < FN, first, second), result)
    grad_ref[...] = result[:, :2 * FN]

    for copy in sent + tgt_copies + c_copies + [n_copies] + p_copies:
        copy.wait_send()
    for copy in outs:
        copy.wait()


def emit(adj_in, grad_in, adj_out, grad_out, sem):
    copies = [
        pltpu.make_async_copy(adj_in, adj_out, sem.at[0]),
        pltpu.make_async_copy(grad_in, grad_out, sem.at[1]),
    ]
    for copy in copies:
        copy.start()
    for copy in copies:
        copy.wait()


def shards(adj_rhs, psi_init, couple, diag_inv, neighbours, sens, owner):
    vmem, dma = pltpu.VMEM, pltpu.SemaphoreType.DMA
    pinned = (pltpu.VMEM((B, FN, R), F32), pltpu.VMEM((8, 2 * FN), F32))
    shapes = (jax.ShapeDtypeStruct((B, FN, R), F32), jax.ShapeDtypeStruct((8, 2 * FN), F32))
    results = pl.pallas_call(
        kernel,
        out_shape=pinned,
        in_specs=[pl.BlockSpec(memory_space=pltpu.HBM)] * 7,
        out_specs=(pl.BlockSpec(memory_space=pl.ANY), pl.BlockSpec(memory_space=pltpu.VMEM)),
        scratch_shapes=[
            vmem((B, FN, R), F32),
            vmem((B, FN, R), F32),
            vmem((B, NBR, R, R), BF),
            vmem((B, R, R), BF),
            pltpu.SMEM((NBR, B), I32),
            vmem((B, KLOC, R), BF),
            vmem((B, KLOC), I32),
            vmem((B, FN, R), F32),
            *[vmem((B, FN, R), BF)] * SWEEPS,
            *[vmem((2, 6, FN, R), BF)] * SWEEPS,
            vmem((R, 256), BF),
            vmem((NZ, 1, 128), I32),
            vmem((NZ * 128, 512), BF),
            vmem((128, 384), BF),
            vmem((NZ, FN, 128), BF),
            vmem((2, FN, 128), F32),
            vmem((2, FN, 128), F32),
            vmem((64, 2, 128), F32),
            vmem((2 * NX * NY, 2, 128), F32),
            dma((7,)), dma((2 * len(GROUPS),)), dma((3,)),
            dma((SWEEPS, 2)), dma((SWEEPS, 2)),
            dma((NZ - 1,)), dma((NZ - 1,)), dma((NZ - 1,)), dma((NZ - 1,)),
            dma((2,)), dma((2,)),
            dma((2 * NX * NY - 1,)), dma((2 * NX * NY - 1,)),
            pltpu.SemaphoreType.REGULAR,
        ],
        compiler_params=pltpu.CompilerParams(
            collective_id=0, has_side_effects=True, vmem_limit_bytes=62 * 2**20
        ),
        name="adjoint_gradient",
    )(adj_rhs, psi_init, couple, diag_inv, neighbours.T, sens, owner)
    return pl.pallas_call(
        emit,
        out_shape=shapes,
        in_specs=[pl.BlockSpec(memory_space=pl.ANY)] * 2,
        out_specs=(pl.BlockSpec(memory_space=pl.ANY),) * 2,
        scratch_shapes=[dma((2,))],
        compiler_params=pltpu.CompilerParams(vmem_limit_bytes=24 * 2**20),
        name="emit",
    )(*results)


def solution(mesh):
    return jax.shard_map(
        shards,
        mesh=mesh,
        in_specs=(
            P("hull", "fn", None),
            P("hull", "fn", None),
            P("hull", None, None, None),
            P("hull", None, None),
            P("hull", None),
            P("hull", None, None),
            P("hull", None),
        ),
        out_specs=(P("hull", "fn", None), P(("hull", "fn"), None)),
        check_vma=False,
    )
```

time: 50.7 us -> 43.7 us (0.86)
  Pallas kernels: 46.9 us -> 42.9 us
  local copies, waits for them, and re-layouts: 2.95 us -> 0 us
    pallas_call x1 -> x2, Pallas kernels: 46.9 us -> 42.9 us  [the longest x1 42.2 us: shards(): pl.pallas_call(kernel, out_shape=pinned, in_specs=[pl.BlockSpec(memory_sp...]
    unnamed x2 -> x0, local copies, waits for them, and re-layouts: 2.95 us -> none
where the time goes in v2:
time: 43.7 us; the launch traced here: 43.6 us
  Pallas kernels  42.9 us (98%)
  between operations  0.64 us (1%)
    pallas_call x1, Pallas kernels, shards(): pl.pallas_call(kernel, out_shape=pinned, in_specs=[pl.BlockSpec(memory_sp...  42.2 us

profile of v2, /device:TPU:1, one launch (start us, length us, event | category | flops | bytes accessed | tf_op | source)
XLA Modules:
  0.0 43.6 jit_solution(6754766751480450663)
XLA Ops:
  0.6 42.2 %adjoint_gradient.1 = (f32[16,32,128]{2,1,0:T(8,128)S(1)}, f32[8,64]{1,0:T(8,128)S(1)}) custom-call(f32[16,32,128]{2,1,0:T(8,128)} %rhs_hbm.1, f32[16,32,128]{2,1,0:T(8,128)} %psi_hbm.1, bf16[16,6,128,128]{3,2,1,0:T(8,128)(2,1)} %couple_hbm.1, bf16[16,128,128]{2,1,0:T(8,128)(2,1)} %diag_hbm.1, s32[6,16]{1,0:T(8,128)} %bitcast.1, ...), custom_call_target="tpu_custom_call" | custom-call | tf_op jit(solution)/shard_map/adjoint_gradient/pallas_call | solution.py:338
  42.8 0.7 %emit.1 = (f32[16,32,128]{2,1,0:T(8,128)}, f32[8,64]{1,0:T(8,128)}) custom-call(f32[16,32,128]{2,1,0:T(8,128)S(1)} %get-tuple-element.4.adj_in, f32[8,64]{1,0:T(8,128)S(1)} %get-tuple-element.5.grad_in), custom_call_target="tpu_custom_call" | custom-call | tf_op jit(solution)/shard_map/emit/pallas_call | solution.py:375

commit v3 on v2

--- a/solution.py
+++ b/solution.py
@@ -16,11 +16,17 @@
 NBR, KLOC, SWEEPS, REACH = 6, 16, 3, 2
 GROUPS = ((2, 6), (6, 10), (10, 14), (0, 2), (14, 16))
 INNER = tuple(range(2, B - 2))
+MIDDLE = tuple(range(4, B - 4))
+BETWEEN = (2, 3, B - 4, B - 3)
 OUTER = (0, 1, B - 2, B - 1)
 
 
 def dot(a, b):
     return jnp.dot(a, b, preferred_element_type=F32)
+
+
+def dot_t(a, b):
+    return lax.dot_general(a, b, (((1,), (1,)), ((), ())), preferred_element_type=F32)
 
 
 def iota(shape, dim):
@@ -31,8 +37,10 @@
     rhs_hbm, psi_hbm, couple_hbm, diag_hbm, nbr_hbm, sens_hbm, owner_hbm,
     adj_hbm, grad_ref,
     rhs, psi, couple, diag, nbr, sens, owner, adj,
-    local0, local1, local2, edge0, edge1, edge2, st, tgt, oh, ohn, crecv, nsend, nrecv, psend, precv,
-    load_sem, weight_sem, out_sem, halo_s, halo_r, tgt_s, tgt_r, c_s, c_r, n_s, n_r, p_s, p_r, plane_sem,
+    local0, local1, local2, edge0, edge1, edge2, part, st, osend, orecv, vsend, vrecv, vt,
+    tgt, oh, ohn, crecv, nsend, nrecv, psend, precv,
+    load_sem, weight_sem, out_sem, halo_s, halo_r, o_s, o_r, v_s, v_r, tgt_s, tgt_r, c_s, c_r, n_s, n_r, p_s, p_r,
+    known1, known2, known3,
 ):
     local, edge = (local0, local1, local2), (edge0, edge1, edge2)
     h = lax.axis_index("hull")
@@ -51,16 +59,27 @@
     plane = [(e, i, k) for e in range(2) for i in range(NX) for k in range(NY) if (e, i, k) != (0, 0, 0)]
     plane.sort(key=lambda t: (-min(t[1], NX - t[1]) - min(t[2], NY - t[2]), -t[0]))
     plane_peers = [device((x + i) % NX, (y + k) % NY, z, (core + e) % 2) for e, i, k in plane]
-    yc_peers = [p for p, (e, i, k) in zip(plane_peers, plane) if i == 0]
+    twin = [(h, 1 - core)]
+
+    def within(n, far):
+        return [k for k in range(1, n) if min(k, n - k) in far]
+
+    def along(far):
+        steps_z = [device(x, y, (z + k) % NZ, core) for k in within(NZ, far)]
+        return steps_z + [device(x, (y + k) % NY, z, core) for k in within(NY, far)]
+
+    def tell(semaphore, peers):
+        for peer in peers:
+            pl.semaphore_signal(semaphore, inc=1, device_id=peer, device_id_type=MESH)
 
     barrier = pltpu.get_barrier_semaphore()
-    everyone = z_peers + x_peers + yc_peers
     for there, peer in ((has_right, right), (has_left, left)):
         @pl.when(there)
         def _():
-            pl.semaphore_signal(barrier, inc=1, device_id=peer, device_id_type=MESH)
-    for peer in everyone:
-        pl.semaphore_signal(barrier, inc=1, device_id=peer, device_id_type=MESH)
+            tell(barrier, [peer])
+    close_peers = along((1, 2)) + x_peers + twin
+    tell(barrier, close_peers)
+    round1, round2, round3 = along((2,)) + twin, x_peers + twin, x_peers
 
     loads = {}
 
@@ -97,8 +116,12 @@
         local[s][i] = value
         if i < 4:
             edge[s][0, i + 2] = value
+            if s == SWEEPS - 1:
+                part[0, i + 2] = value
         if i >= B - 4:
             edge[s][1, i - (B - 4)] = value
+            if s == SWEEPS - 1:
+                part[1, i - (B - 4)] = value
 
     class Pair:
         def __init__(self, sources, targets, send, recv):
@@ -149,14 +172,20 @@
         for ref in edge:
             ref[0, 0:2] = jnp.zeros((2, FN, R), BF)
         nrecv[0] = jnp.zeros((FN, 128), F32)
+        orecv[0] = jnp.full((1, 128), -1, I32)
+        vrecv[0] = jnp.zeros((32, 256), BF)
 
     @pl.when(jnp.logical_not(has_right))
     def _():
         for ref in edge:
             ref[1, 4:6] = jnp.zeros((2, FN, R), BF)
         nrecv[1] = jnp.zeros((FN, 128), F32)
-
-    sent = []
+        orecv[1] = jnp.full((1, 128), -1, I32)
+        vrecv[1] = jnp.zeros((32, 256), BF)
+
+    part[0, 0:2] = jnp.zeros((2, FN, R), BF)
+    part[1, 4:6] = jnp.zeros((2, FN, R), BF)
+
     loads["psi0"].wait()
     loads["psi1"].wait()
     for i in (0, 1, B - 2, B - 1):
@@ -167,19 +196,19 @@
     high = (owners >> 6).astype(F32).astype(BF)
     low = (owners & 63).astype(F32).astype(BF)
 
-    def owner_row(first):
-        pick = jnp.where(slot == first + (lane & 7), 1.0, 0.0).astype(BF)
+    def owner_row(block_row, block_slot):
+        pick = jnp.where(slot == block_slot, 1.0, 0.0).astype(BF)
         spread = dot(high, pick) * 64.0 + dot(low, pick)
-        return jnp.sum(jnp.where(slot == lane >> 3, spread, 0.0), axis=0, keepdims=True).astype(I32)
-
-    tgt[0] = owner_row(8)
-    near_owner = owner_row(0)
-
-    pl.semaphore_wait(barrier, len(everyone) + has_right.astype(I32) + has_left.astype(I32))
-    for peer in x_peers:
-        pl.semaphore_signal(plane_sem, inc=1, device_id=peer, device_id_type=MESH)
+        return jnp.sum(jnp.where(slot == block_row, spread, 0.0), axis=0, keepdims=True).astype(I32)
+
+    far_owner = owner_row(lane >> 3, 8 + (lane & 7))
+    near_owner = owner_row(lane >> 3, lane & 7)
+    osend[...] = owner_row(jnp.where((lane & 63) < 32, B - 2, 0) + ((lane >> 4) & 1), lane & 15)
+
+    pl.semaphore_wait(barrier, len(close_peers) + has_right.astype(I32) + has_left.astype(I32))
     halo = send_halo(0)
-    tgt_copies = [remote(tgt.at[0], tgt.at[k], tgt_s.at[k - 1], tgt_r.at[k - 1], p) for k, p in zip(z_steps, z_peers)]
+    o_copies = Pair((osend, osend), (orecv.at[0], orecv.at[1]), (o_s.at[0], o_s.at[1]), (o_r.at[0], o_r.at[1]))
+    tell(known1, round1)
 
     loads["psi"].wait()
     for i in range(2, B - 2):
@@ -192,16 +221,17 @@
             updated.append((rhs[i] - dot(nearby, couple[i].reshape(NBR * R, R))).astype(BF))
         return [dot(u, diag[i]) for u, i in zip(updated, rows)]
 
-    def interior(s):
-        return blocks(s, INNER, lambda i, p: local[s][jnp.clip(p, 0, B - 1)])
+    def from_local(s, i, p):
+        return local[s][jnp.clip(p, 0, B - 1)]
+
+    def interior(s, rows):
+        return blocks(s, rows, lambda i, p: from_local(s, i, p))
+
+    def from_edge(ref, i, p):
+        return ref[0, jnp.clip(p + 2, 0, 5)] if i < 2 else ref[1, jnp.clip(p - (B - 4), 0, 5)]
 
     def boundary(s):
-        def read(i, p):
-            if i < 2:
-                return edge[s][0, jnp.clip(p + 2, 0, 5)]
-            return edge[s][1, jnp.clip(p - (B - 4), 0, 5)]
-
-        return blocks(s, OUTER, read)
+        return blocks(s, OUTER, lambda i, p: from_edge(edge[s], i, p))
 
     outs = []
 
@@ -220,13 +250,13 @@
     for group in weights:
         for copy in group:
             copy.wait()
-    for i, value in zip(INNER, interior(0)):
+    for i, value in zip(INNER, interior(0, INNER)):
         keep(1, i, value.astype(BF))
     loads["sens"].wait()
     wide = sens[...].astype(F32)
     for q, first in enumerate((8, 0)):
-        part = wide[:, first:first + 8, :].reshape(128, R)
-        st[:, q * 128:(q + 1) * 128] = (-jnp.transpose(part)).astype(BF)
+        chunk = wide[:, first:first + 8, :].reshape(128, R)
+        st[:, q * 128:(q + 1) * 128] = (-jnp.transpose(chunk)).astype(BF)
     block_of = near_owner >> 4
     group = jnp.where(block_of == h, 0, jnp.where(block_of == h - 1, 128, 256))
     place = group + (near_owner & 3) * 32 + ((near_owner >> 3) & 1) * 2 + ((near_owner >> 2) & 1)
@@ -234,57 +264,104 @@
     column = jnp.transpose(jnp.broadcast_to(place, (8, 128)).astype(F32))[:, :1].astype(I32)
     ohn[...] = jnp.where(column == iota((128, 384), 1), 1.0, 0.0).astype(BF)
 
-    for s in range(SWEEPS):
-        last = s == SWEEPS - 1
-        halo.wait_recv()
-        sent.append(halo)
-        values = boundary(s)
-        if last:
-            break
-        for i, value in zip(OUTER, values):
-            keep(s + 1, i, value.astype(BF))
-        halo = send_halo(s + 1)
-        inner = interior(s + 1)
-        if s + 1 < SWEEPS - 1:
-            for i, value in zip(INNER, inner):
-                keep(s + 2, i, value.astype(BF))
-            for copy in tgt_copies:
-                copy.wait_recv()
-            rows = jnp.concatenate([tgt[k] for k in range(NZ)], axis=0)
-            hull = rows >> 4
-            place = (rows & 3) * 128 + (hull // NZ) * 4 + ((rows >> 3) & 1) * 2 + ((rows >> 2) & 1)
-            place = jnp.where(hull % NZ == z, place, -1)
-            if NZ < 8:
-                place = jnp.concatenate([place] * (8 // NZ), axis=0)
-            columns = jnp.transpose(place.astype(F32)).astype(I32)
-            for k in range(NZ):
-                oh[k * 128:(k + 1) * 128, :] = jnp.where(columns[:, k:k + 1] == iota((128, 512), 1), 1.0, 0.0).astype(BF)
-        else:
-            for i, value in zip(INNER, inner):
-                adj[i] = value
-            put(2, B - 2)
-            terms = contributions(INNER, inner)
-    terms = terms + contributions(OUTER, values)
-
-    terms = terms.astype(BF)
-    crecv[0] = terms[:, :128]
+    for side, (rows, others) in enumerate((((B - 2, B - 1), (B, B + 1)), ((0, 1), (-2, -1)))):
+        for n, i in enumerate(rows):
+            shape = dot_t(sens[i], diag[i]).astype(BF)
+            slots = dot_t(shape, couple[i].reshape(NBR * R, R))
+            for m, j in enumerate(others):
+                vsend[side, n * KLOC:(n + 1) * KLOC, m * R:(m + 1) * R] = sum(
+                    jnp.where(nbr[k, i] - h * B == j, slots[:, k * R:(k + 1) * R], 0.0) for k in range(NBR)
+                ).astype(BF)
+    v_copies = Pair(*[(ref.at[0], ref.at[1]) for ref in (vsend, vrecv, v_s, v_r)])
+
+    pl.semaphore_wait(known1, len(round1))
+    tell(known2, round2)
+    o_copies.wait_recv()
+    lane = iota((1, 128), 1)
+    tgt[0] = jnp.concatenate([far_owner, jnp.where((lane & 63) < 32, orecv[0], orecv[1])], axis=0)
+    tgt_copies = [
+        remote(tgt.at[0], tgt.at[k], tgt_s.at[k - 1], tgt_r.at[k - 1], p) for k, p in zip(z_steps, z_peers)
+    ]
+
+    halo.wait_recv()
+    sent = [halo, o_copies, v_copies]
+    for i, value in zip(OUTER, boundary(0)):
+        keep(1, i, value.astype(BF))
+    halo = send_halo(1)
+    for i, value in zip(INNER, interior(1, INNER)):
+        keep(2, i, value.astype(BF))
+    values = interior(2, MIDDLE)
+    for i, value in zip(MIDDLE, values):
+        adj[i] = value
+    put(MIDDLE[0], MIDDLE[-1] + 1)
+    terms = contributions(MIDDLE, values)
+    pl.semaphore_wait(known2, len(round2))
+    tell(known3, round3)
+    v_copies.wait_recv()
+    zero = jnp.zeros((32, 256), F32)
+    vt[...] = jnp.transpose(
+        jnp.concatenate(
+            [
+                jnp.concatenate([vrecv[0].astype(F32), zero], axis=1),
+                jnp.concatenate([zero, vrecv[1].astype(F32)], axis=1),
+                jnp.zeros((64, 512), F32),
+            ],
+            axis=0,
+        )
+    ).astype(BF)
+
+    halo.wait_recv()
+    sent.append(halo)
+    for i, value in zip(OUTER, boundary(1)):
+        keep(2, i, value.astype(BF))
+    halo = send_halo(2)
+    sent.append(halo)
+
+    rows = BETWEEN + OUTER
+    values = blocks(2, rows, lambda i, p: from_edge(part, i, p) if i in OUTER else from_local(2, i, p))
+    terms = (terms + contributions(rows, values)).astype(BF)
+    beyond = dot(jnp.concatenate([local[2][i] for i in OUTER], axis=1), vt[...])
+    lane = iota((16, 128), 1)
+    crecv[0, 0:FN] = terms[:, :128]
+    crecv[0, FN:48] = jnp.where(lane < 64, beyond[:16], pltpu.roll(beyond[16:], 64, 1)).astype(BF)
+
     c_copies = [remote(crecv.at[0], crecv.at[k], c_s.at[k - 1], c_r.at[k - 1], p) for k, p in zip(z_steps, z_peers)]
     close = dot(terms[:, 128:], ohn[...])
     nsend[0] = close[:, 256:]
     nsend[1] = close[:, 128:256]
     n_copies = Pair(*[(ref.at[0], ref.at[1]) for ref in (nsend, nrecv, n_s, n_r)])
-    for i, value in zip(OUTER, values):
+    for i, value in zip(BETWEEN, values):
         adj[i] = value
-    put(0, 2)
-    put(B - 2, B)
+    put(2, 4)
+    put(B - 4, B - 2)
+    for copy in tgt_copies:
+        copy.wait_recv()
+    for n in range(2):
+        rows = jnp.concatenate([tgt[k, n:n + 1] for k in range(NZ)], axis=0)
+        hull = rows >> 4
+        place = (rows & 3) * 128 + (hull // NZ) * 4 + ((rows >> 3) & 1) * 2 + ((rows >> 2) & 1)
+        place = jnp.where((hull % NZ == z) & (rows >= 0), place, -1)
+        if NZ < 8:
+            place = jnp.concatenate([place] * (8 // NZ), axis=0)
+        columns = jnp.transpose(place.astype(F32)).astype(I32)
+        for k in range(NZ):
+            oh[(n * NZ + k) * 128:(n * NZ + k + 1) * 128, :] = jnp.where(
+                columns[:, k:k + 1] == iota((128, 512), 1), 1.0, 0.0
+            ).astype(BF)
     n_copies.wait_recv()
     close = close[:, :128] + nrecv[0] + nrecv[1]
     stacked = jnp.concatenate([close if g == 0 else pltpu.roll(close, 128 - 32 * g, 1) for g in range(4)], axis=0)
     close = jnp.transpose(stacked)[:4, :]
-    pl.semaphore_wait(plane_sem, NX - 1)
+    pl.semaphore_wait(known3, len(round3))
     for copy in c_copies:
         copy.wait_recv()
-    dense = dot(jnp.concatenate([crecv[k] for k in range(NZ)], axis=1), oh[...])
+    lane = iota((16, 128), 1)
+    extra = []
+    for k in range(NZ):
+        both = crecv[k, FN:48].astype(F32)
+        halves = [jnp.where(lane < 64, both, 0.0), jnp.where(lane < 64, 0.0, both)]
+        extra.append(jnp.concatenate(halves, axis=0).astype(BF))
+    dense = dot(jnp.concatenate([crecv[k, 0:FN] for k in range(NZ)] + extra, axis=1), oh[...])
 
     packed = jnp.transpose(jnp.concatenate([dense[:, g * 128:(g + 1) * 128] for g in range(4)], axis=0))
     for d in range(2 * NX * NY):
@@ -300,6 +377,11 @@
         for n, (e, i, k) in enumerate(plane)
     ]
     own = psend[mine + core]
+    halo.wait_recv()
+    for i, value in zip(OUTER, boundary(2)):
+        adj[i] = value
+    put(0, 2)
+    put(B - 2, B)
     for copy in p_copies:
         copy.wait_recv()
     half = NX * NY
@@ -351,21 +433,28 @@
             vmem((B, FN, R), F32),
             *[vmem((B, FN, R), BF)] * SWEEPS,
             *[vmem((2, 6, FN, R), BF)] * SWEEPS,
+            vmem((2, 6, FN, R), BF),
             vmem((R, 256), BF),
-            vmem((NZ, 1, 128), I32),
-            vmem((NZ * 128, 512), BF),
+            vmem((1, 128), I32),
+            vmem((2, 1, 128), I32),
+            vmem((2, 32, 256), BF),
+            vmem((2, 32, 256), BF),
+            vmem((512, 128), BF),
+            vmem((NZ, 2, 128), I32),
+            vmem((2 * NZ * 128, 512), BF),
             vmem((128, 384), BF),
-            vmem((NZ, FN, 128), BF),
+            vmem((NZ, 48, 128), BF),
             vmem((2, FN, 128), F32),
             vmem((2, FN, 128), F32),
             vmem((64, 2, 128), F32),
             vmem((2 * NX * NY, 2, 128), F32),
-            dma((7,)), dma((2 * len(GROUPS),)), dma((3,)),
+            dma((7,)), dma((2 * len(GROUPS),)), dma((5,)),
             dma((SWEEPS, 2)), dma((SWEEPS, 2)),
+            dma((2,)), dma((2,)), dma((2,)), dma((2,)),
             dma((NZ - 1,)), dma((NZ - 1,)), dma((NZ - 1,)), dma((NZ - 1,)),
             dma((2,)), dma((2,)),
             dma((2 * NX * NY - 1,)), dma((2 * NX * NY - 1,)),
-            pltpu.SemaphoreType.REGULAR,
+            *[pltpu.SemaphoreType.REGULAR] * 3,
         ],
         compiler_params=pltpu.CompilerParams(
             collective_id=0, has_side_effects=True, vmem_limit_bytes=62 * 2**20

time: 43.7 us -> 39.9 us (0.913)
  Pallas kernels: 42.9 us -> 39.1 us
    pallas_call x1, Pallas kernels: 42.2 us -> 38.4 us  [shards(): pl.pallas_call(kernel, out_shape=pinned, in_specs=[pl.BlockSpec(memory_sp...]
where the time goes in v3:
time: 39.9 us; the launch traced here: 39.7 us
  Pallas kernels  39.1 us (98%)
  between operations  0.64 us (2%)
    pallas_call x1, Pallas kernels, shards(): pl.pallas_call(kernel, out_shape=pinned, in_specs=[pl.BlockSpec(memory_sp...  38.4 us

profile of v3, /device:TPU:1, one launch (start us, length us, event | category | flops | bytes accessed | tf_op | source)
XLA Modules:
  0.0 39.7 jit_solution(411921507313794305)
XLA Ops:
  0.6 38.4 %adjoint_gradient.1 = (f32[16,32,128]{2,1,0:T(8,128)S(1)}, f32[8,64]{1,0:T(8,128)S(1)}) custom-call(f32[16,32,128]{2,1,0:T(8,128)} %rhs_hbm.1, f32[16,32,128]{2,1,0:T(8,128)} %psi_hbm.1, bf16[16,6,128,128]{3,2,1,0:T(8,128)(2,1)} %couple_hbm.1, bf16[16,128,128]{2,1,0:T(8,128)(2,1)} %diag_hbm.1, s32[6,16]{1,0:T(8,128)} %bitcast.1, ...), custom_call_target="tpu_custom_call" | custom-call | tf_op jit(solution)/shard_map/adjoint_gradient/pallas_call | solution.py:420
  39.0 0.7 %emit.1 = (f32[16,32,128]{2,1,0:T(8,128)}, f32[8,64]{1,0:T(8,128)}) custom-call(f32[16,32,128]{2,1,0:T(8,128)S(1)} %get-tuple-element.4.adj_in, f32[8,64]{1,0:T(8,128)S(1)} %get-tuple-element.5.grad_in), custom_call_target="tpu_custom_call" | custom-call | tf_op jit(solution)/shard_map/emit/pallas_call | solution.py:464

commit v4 on v3

--- a/solution.py
+++ b/solution.py
@@ -171,7 +171,6 @@
     def _():
         for ref in edge:
             ref[0, 0:2] = jnp.zeros((2, FN, R), BF)
-        nrecv[0] = jnp.zeros((FN, 128), F32)
         orecv[0] = jnp.full((1, 128), -1, I32)
         vrecv[0] = jnp.zeros((32, 256), BF)
 
@@ -179,9 +178,14 @@
     def _():
         for ref in edge:
             ref[1, 4:6] = jnp.zeros((2, FN, R), BF)
-        nrecv[1] = jnp.zeros((FN, 128), F32)
         orecv[1] = jnp.full((1, 128), -1, I32)
         vrecv[1] = jnp.zeros((32, 256), BF)
+
+    near_arrives = jnp.where(core == 1, has_right, has_left)
+
+    @pl.when(jnp.logical_not(near_arrives))
+    def _():
+        nrecv[...] = jnp.zeros((2, 2, 128), F32)
 
     part[0, 0:2] = jnp.zeros((2, FN, R), BF)
     part[1, 4:6] = jnp.zeros((2, FN, R), BF)
@@ -258,11 +262,11 @@
         chunk = wide[:, first:first + 8, :].reshape(128, R)
         st[:, q * 128:(q + 1) * 128] = (-jnp.transpose(chunk)).astype(BF)
     block_of = near_owner >> 4
-    group = jnp.where(block_of == h, 0, jnp.where(block_of == h - 1, 128, 256))
+    group = jnp.where(block_of == h, 0, jnp.where(block_of == h - 1, 4, 8))
     place = group + (near_owner & 3) * 32 + ((near_owner >> 3) & 1) * 2 + ((near_owner >> 2) & 1)
     place = jnp.where(jnp.abs(block_of - h) <= 1, place, -1)
     column = jnp.transpose(jnp.broadcast_to(place, (8, 128)).astype(F32))[:, :1].astype(I32)
-    ohn[...] = jnp.where(column == iota((128, 384), 1), 1.0, 0.0).astype(BF)
+    ohn[...] = jnp.where(column == iota((128, 128), 1), 1.0, 0.0).astype(BF)
 
     for side, (rows, others) in enumerate((((B - 2, B - 1), (B, B + 1)), ((0, 1), (-2, -1)))):
         for n, i in enumerate(rows):
@@ -274,6 +278,11 @@
                 ).astype(BF)
     v_copies = Pair(*[(ref.at[0], ref.at[1]) for ref in (vsend, vrecv, v_s, v_r)])
 
+    halo.wait_recv()
+    sent = [halo, o_copies, v_copies]
+    for i, value in zip(OUTER, boundary(0)):
+        keep(1, i, value.astype(BF))
+    halo = send_halo(1)
     pl.semaphore_wait(known1, len(round1))
     tell(known2, round2)
     o_copies.wait_recv()
@@ -283,11 +292,6 @@
         remote(tgt.at[0], tgt.at[k], tgt_s.at[k - 1], tgt_r.at[k - 1], p) for k, p in zip(z_steps, z_peers)
     ]
 
-    halo.wait_recv()
-    sent = [halo, o_copies, v_copies]
-    for i, value in zip(OUTER, boundary(0)):
-        keep(1, i, value.astype(BF))
-    halo = send_halo(1)
     for i, value in zip(INNER, interior(1, INNER)):
         keep(2, i, value.astype(BF))
     values = interior(2, MIDDLE)
@@ -315,7 +319,6 @@
     for i, value in zip(OUTER, boundary(1)):
         keep(2, i, value.astype(BF))
     halo = send_halo(2)
-    sent.append(halo)
 
     rows = BETWEEN + OUTER
     values = blocks(2, rows, lambda i, p: from_edge(part, i, p) if i in OUTER else from_local(2, i, p))
@@ -327,9 +330,21 @@
 
     c_copies = [remote(crecv.at[0], crecv.at[k], c_s.at[k - 1], c_r.at[k - 1], p) for k, p in zip(z_steps, z_peers)]
     close = dot(terms[:, 128:], ohn[...])
-    nsend[0] = close[:, 256:]
-    nsend[1] = close[:, 128:256]
-    n_copies = Pair(*[(ref.at[0], ref.at[1]) for ref in (nsend, nrecv, n_s, n_r)])
+    stacked = jnp.concatenate([close if g == 0 else pltpu.roll(close, 128 - 32 * g, 1) for g in range(4)], axis=0)
+    close = jnp.transpose(stacked)[:16, :]
+    nsend[0] = close[6:8, :]
+    nsend[1] = close[8:10, :]
+    n_copies = [
+        pltpu.make_async_remote_copy(
+            src_ref=nsend.at[k], dst_ref=nrecv.at[core], send_sem=n_s.at[k], recv_sem=n_r.at[core],
+            device_id=peer, device_id_type=MESH,
+        )
+        for k, peer in enumerate(((left[0], 1), (right[0], 0)))
+    ]
+    for there, copy in zip((has_left, has_right), n_copies):
+        @pl.when(there)
+        def _():
+            copy.start()
     for i, value in zip(BETWEEN, values):
         adj[i] = value
     put(2, 4)
@@ -345,23 +360,21 @@
             place = jnp.concatenate([place] * (8 // NZ), axis=0)
         columns = jnp.transpose(place.astype(F32)).astype(I32)
         for k in range(NZ):
-            oh[(n * NZ + k) * 128:(n * NZ + k + 1) * 128, :] = jnp.where(
+            oh[(2 * k + n) * 128:(2 * k + n + 1) * 128, :] = jnp.where(
                 columns[:, k:k + 1] == iota((128, 512), 1), 1.0, 0.0
             ).astype(BF)
-    n_copies.wait_recv()
-    close = close[:, :128] + nrecv[0] + nrecv[1]
-    stacked = jnp.concatenate([close if g == 0 else pltpu.roll(close, 128 - 32 * g, 1) for g in range(4)], axis=0)
-    close = jnp.transpose(stacked)[:4, :]
     pl.semaphore_wait(known3, len(round3))
-    for copy in c_copies:
-        copy.wait_recv()
     lane = iota((16, 128), 1)
-    extra = []
-    for k in range(NZ):
+    dense = None
+    arrivals = [None] + c_copies[::-1]
+    for k, copy in zip([0] + z_steps[::-1], arrivals):
+        if copy is not None:
+            copy.wait_recv()
         both = crecv[k, FN:48].astype(F32)
-        halves = [jnp.where(lane < 64, both, 0.0), jnp.where(lane < 64, 0.0, both)]
-        extra.append(jnp.concatenate(halves, axis=0).astype(BF))
-    dense = dot(jnp.concatenate([crecv[k, 0:FN] for k in range(NZ)] + extra, axis=1), oh[...])
+        extra = jnp.concatenate([jnp.where(lane < 64, both, 0.0), jnp.where(lane < 64, 0.0, both)], axis=0)
+        terms = jnp.concatenate([crecv[k, 0:FN], extra.astype(BF)], axis=1)
+        product = dot(terms, oh[k * 256:(k + 1) * 256, :])
+        dense = product if dense is None else dense + product
 
     packed = jnp.transpose(jnp.concatenate([dense[:, g * 128:(g + 1) * 128] for g in range(4)], axis=0))
     for d in range(2 * NX * NY):
@@ -377,16 +390,37 @@
         for n, (e, i, k) in enumerate(plane)
     ]
     own = psend[mine + core]
+    for copy in sent + tgt_copies + c_copies:
+        copy.wait_send()
+    for there, copy in zip((has_left, has_right), n_copies):
+        @pl.when(there)
+        def _():
+            copy.wait_send()
+
+    @pl.when(near_arrives)
+    def _():
+        for k in range(2):
+            pltpu.make_async_remote_copy(
+                src_ref=nsend.at[k], dst_ref=nrecv.at[k], send_sem=n_s.at[k], recv_sem=n_r.at[k],
+                device_id=twin[0], device_id_type=MESH,
+            ).wait_recv()
+
     halo.wait_recv()
     for i, value in zip(OUTER, boundary(2)):
         adj[i] = value
     put(0, 2)
     put(B - 2, B)
+    halo.wait_send()
     for copy in p_copies:
+        copy.wait_send()
+    for copy in p_copies[::-1]:
         copy.wait_recv()
     half = NX * NY
     halves = [own + jnp.sum(precv[1:half], axis=0), jnp.sum(precv[half:2 * half], axis=0)]
-    ordered = (jnp.where(core == 0, halves[0], halves[1]), jnp.where(core == 0, halves[1], halves[0]))
+    ordered = (
+        jnp.where(core == 0, halves[0], halves[1]) + nrecv[0],
+        jnp.where(core == 0, halves[1], halves[0]) + nrecv[1],
+    )
     row, lane = iota((8, 128), 0), iota((8, 128), 1)
     wide = [jnp.where(row < 4, half[0:1], half[1:2]) for half in ordered]
     result = jnp.zeros((8, 128), F32)
@@ -396,8 +430,6 @@
         result = jnp.where((row & 3) == g, jnp.where(lane < FN, first, second), result)
     grad_ref[...] = result[:, :2 * FN]
 
-    for copy in sent + tgt_copies + c_copies + [n_copies] + p_copies:
-        copy.wait_send()
     for copy in outs:
         copy.wait()
 
@@ -442,10 +474,10 @@
             vmem((512, 128), BF),
             vmem((NZ, 2, 128), I32),
             vmem((2 * NZ * 128, 512), BF),
-            vmem((128, 384), BF),
+            vmem((128, 128), BF),
             vmem((NZ, 48, 128), BF),
-            vmem((2, FN, 128), F32),
-            vmem((2, FN, 128), F32),
+            vmem((2, 2, 128), F32),
+            vmem((2, 2, 128), F32),
             vmem((64, 2, 128), F32),
             vmem((2 * NX * NY, 2, 128), F32),
             dma((7,)), dma((2 * len(GROUPS),)), dma((5,)),

time: 39.9 us -> 37.7 us (0.945)
  Pallas kernels: 39.1 us -> 36.9 us
    pallas_call x1, Pallas kernels: 38.4 us -> 36.2 us  [shards(): pl.pallas_call(kernel, out_shape=pinned, in_specs=[pl.BlockSpec(memory_sp...]
where the time goes in v4:
time: 37.7 us; the launch traced here: 37.6 us
  Pallas kernels  36.9 us (98%)
  between operations  0.64 us (2%)
    pallas_call x1, Pallas kernels, shards(): pl.pallas_call(kernel, out_shape=pinned, in_specs=[pl.BlockSpec(memory_sp...  36.2 us

profile of v4, /device:TPU:1, one launch (start us, length us, event | category | flops | bytes accessed | tf_op | source)
XLA Modules:
  0.0 37.6 jit_solution(8576930391182429401)
XLA Ops:
  0.6 36.2 %adjoint_gradient.1 = (f32[16,32,128]{2,1,0:T(8,128)S(1)}, f32[8,64]{1,0:T(8,128)S(1)}) custom-call(f32[16,32,128]{2,1,0:T(8,128)} %rhs_hbm.1, f32[16,32,128]{2,1,0:T(8,128)} %psi_hbm.1, bf16[16,6,128,128]{3,2,1,0:T(8,128)(2,1)} %couple_hbm.1, bf16[16,128,128]{2,1,0:T(8,128)(2,1)} %diag_hbm.1, s32[6,16]{1,0:T(8,128)} %bitcast.1, ...), custom_call_target="tpu_custom_call" | custom-call | tf_op jit(solution)/shard_map/adjoint_gradient/pallas_call | solution.py:452
  36.9 0.7 %emit.1 = (f32[16,32,128]{2,1,0:T(8,128)}, f32[8,64]{1,0:T(8,128)}) custom-call(f32[16,32,128]{2,1,0:T(8,128)S(1)} %get-tuple-element.4.adj_in, f32[8,64]{1,0:T(8,128)S(1)} %get-tuple-element.5.grad_in), custom_call_target="tpu_custom_call" | custom-call | tf_op jit(solution)/shard_map/emit/pallas_call | solution.py:496

commit v5 on v4

--- a/solution.py
+++ b/solution.py
@@ -40,7 +40,7 @@
     local0, local1, local2, edge0, edge1, edge2, part, st, osend, orecv, vsend, vrecv, vt,
     tgt, oh, ohn, crecv, nsend, nrecv, psend, precv,
     load_sem, weight_sem, out_sem, halo_s, halo_r, o_s, o_r, v_s, v_r, tgt_s, tgt_r, c_s, c_r, n_s, n_r, p_s, p_r,
-    known1, known2, known3,
+    known1, known2, known3, known4,
 ):
     local, edge = (local0, local1, local2), (edge0, edge1, edge2)
     h = lax.axis_index("hull")
@@ -77,9 +77,10 @@
         @pl.when(there)
         def _():
             tell(barrier, [peer])
-    close_peers = along((1, 2)) + x_peers + twin
+    next_peers = along((1,)) + [device((x + k) % NX, y, z, core) for k in within(NX, (1,))]
+    close_peers = next_peers + twin
     tell(barrier, close_peers)
-    round1, round2, round3 = along((2,)) + twin, x_peers + twin, x_peers
+    round1, round2, round3, round4 = next_peers, along((2,)) + twin, x_peers + twin, x_peers
 
     loads = {}
 
@@ -278,20 +279,13 @@
                 ).astype(BF)
     v_copies = Pair(*[(ref.at[0], ref.at[1]) for ref in (vsend, vrecv, v_s, v_r)])
 
+    pl.semaphore_wait(known1, len(round1))
+    tell(known2, round2)
     halo.wait_recv()
     sent = [halo, o_copies, v_copies]
     for i, value in zip(OUTER, boundary(0)):
         keep(1, i, value.astype(BF))
     halo = send_halo(1)
-    pl.semaphore_wait(known1, len(round1))
-    tell(known2, round2)
-    o_copies.wait_recv()
-    lane = iota((1, 128), 1)
-    tgt[0] = jnp.concatenate([far_owner, jnp.where((lane & 63) < 32, orecv[0], orecv[1])], axis=0)
-    tgt_copies = [
-        remote(tgt.at[0], tgt.at[k], tgt_s.at[k - 1], tgt_r.at[k - 1], p) for k, p in zip(z_steps, z_peers)
-    ]
-
     for i, value in zip(INNER, interior(1, INNER)):
         keep(2, i, value.astype(BF))
     values = interior(2, MIDDLE)
@@ -299,8 +293,6 @@
         adj[i] = value
     put(MIDDLE[0], MIDDLE[-1] + 1)
     terms = contributions(MIDDLE, values)
-    pl.semaphore_wait(known2, len(round2))
-    tell(known3, round3)
     v_copies.wait_recv()
     zero = jnp.zeros((32, 256), F32)
     vt[...] = jnp.transpose(
@@ -314,11 +306,19 @@
         )
     ).astype(BF)
 
+    pl.semaphore_wait(known2, len(round2))
+    tell(known3, round3)
+    o_copies.wait_recv()
+    lane = iota((1, 128), 1)
+    tgt[0] = jnp.concatenate([far_owner, jnp.where((lane & 63) < 32, orecv[0], orecv[1])], axis=0)
+    tgt_copies = [
+        remote(tgt.at[0], tgt.at[k], tgt_s.at[k - 1], tgt_r.at[k - 1], p) for k, p in zip(z_steps, z_peers)
+    ]
+
     halo.wait_recv()
     sent.append(halo)
     for i, value in zip(OUTER, boundary(1)):
         keep(2, i, value.astype(BF))
-    halo = send_halo(2)
 
     rows = BETWEEN + OUTER
     values = blocks(2, rows, lambda i, p: from_edge(part, i, p) if i in OUTER else from_local(2, i, p))
@@ -345,10 +345,13 @@
         @pl.when(there)
         def _():
             copy.start()
+    halo = send_halo(2)
     for i, value in zip(BETWEEN, values):
         adj[i] = value
     put(2, 4)
     put(B - 4, B - 2)
+    pl.semaphore_wait(known3, len(round3))
+    tell(known4, round4)
     for copy in tgt_copies:
         copy.wait_recv()
     for n in range(2):
@@ -363,7 +366,6 @@
             oh[(2 * k + n) * 128:(2 * k + n + 1) * 128, :] = jnp.where(
                 columns[:, k:k + 1] == iota((128, 512), 1), 1.0, 0.0
             ).astype(BF)
-    pl.semaphore_wait(known3, len(round3))
     lane = iota((16, 128), 1)
     dense = None
     arrivals = [None] + c_copies[::-1]
@@ -382,6 +384,7 @@
     mine = (x * NY + y) * 2
     psend[mine] += close[0:2, :]
     psend[mine + 1] += close[2:4, :]
+    pl.semaphore_wait(known4, len(round4))
     p_copies = [
         remote(
             psend.at[(((x + i) % NX) * NY + (y + k) % NY) * 2 + (core + e) % 2],
@@ -486,7 +489,7 @@
             dma((NZ - 1,)), dma((NZ - 1,)), dma((NZ - 1,)), dma((NZ - 1,)),
             dma((2,)), dma((2,)),
             dma((2 * NX * NY - 1,)), dma((2 * NX * NY - 1,)),
-            *[pltpu.SemaphoreType.REGULAR] * 3,
+            *[pltpu.SemaphoreType.REGULAR] * 4,
         ],
         compiler_params=pltpu.CompilerParams(
             collective_id=0, has_side_effects=True, vmem_limit_bytes=62 * 2**20

time: 37.7 us -> 37.4 us (level)
  no operation moved by 1% of the time
where the time goes in v5:
time: 37.4 us; the launch traced here: 37.3 us
  Pallas kernels  36.7 us (98%)
  between operations  0.64 us (2%)
    pallas_call x1, Pallas kernels, shards(): pl.pallas_call(kernel, out_shape=pinned, in_specs=[pl.BlockSpec(memory_sp...  36 us

profile of v5, /device:TPU:1, one launch (start us, length us, event | category | flops | bytes accessed | tf_op | source)
XLA Modules:
  0.0 37.3 jit_solution(7898091041666598427)
XLA Ops:
  0.6 36.0 %adjoint_gradient.1 = (f32[16,32,128]{2,1,0:T(8,128)S(1)}, f32[8,64]{1,0:T(8,128)S(1)}) custom-call(f32[16,32,128]{2,1,0:T(8,128)} %rhs_hbm.1, f32[16,32,128]{2,1,0:T(8,128)} %psi_hbm.1, bf16[16,6,128,128]{3,2,1,0:T(8,128)(2,1)} %couple_hbm.1, bf16[16,128,128]{2,1,0:T(8,128)(2,1)} %diag_hbm.1, s32[6,16]{1,0:T(8,128)} %bitcast.1, ...), custom_call_target="tpu_custom_call" | custom-call | tf_op jit(solution)/shard_map/adjoint_gradient/pallas_call | solution.py:455
  36.6 0.7 %emit.1 = (f32[16,32,128]{2,1,0:T(8,128)}, f32[8,64]{1,0:T(8,128)}) custom-call(f32[16,32,128]{2,1,0:T(8,128)S(1)} %get-tuple-element.4.adj_in, f32[8,64]{1,0:T(8,128)S(1)} %get-tuple-element.5.grad_in), custom_call_target="tpu_custom_call" | custom-call | tf_op jit(solution)/shard_map/emit/pallas_call | solution.py:499
